TPU v7x, 32 devices: a whole 2x2x4 slice. The times are simulated.
32 devices in a mesh: group: 2 (over y), atom: 8 (over z, x), wave: 2 (over core).
Axes of the slice: x: 2, y: 2, z: 4, core: 2. Of those that a mesh axis runs over, the one named last changes fastest.
Arguments:
- positions: float32 [3, 16384], P(None, ('group', 'atom')), parts along dimension 1, may hold values from 0 to 64
- features: bfloat16 [16384, 256], P(('group', 'atom')), parts along dimension 0, may hold values from -6 to 6
- cotangent: bfloat16 [16384, 256], P(('group', 'atom')), parts along dimension 0, may hold values from -6 to 6
- filters: float32 [4096, 256], P('wave'), may hold values from -12 to 12
- wave_ints: int32 [3, 4096], P(None, 'wave'), may hold values from -12 to 12, as said below
Outputs:
- grad_features: float32 [16384, 256], P(('group', 'atom', 'wave')), parts along dimension 0
- grad_positions: float32 [3, 16384], P(None, ('group', 'atom', 'wave')), parts along dimension 1
- grad_filter: float32 [8192, 256], P(('group', 'wave')), parts along dimension 0
There are 2 independent parts, one for each index of `group`. A program takes and returns all parts, laid end to end along the dimension named above; an argument that names none is the same for every part. Nothing has to cross between parts.
Inputs may be any that keep to these rules, and one draw needn't show every extreme that they name: `wave_ints`: the 4096 index triples are distinct and nonzero, and all lie in one half-space: first component positive, or first component zero and second positive, or the first two zero and the third positive; so no wavevector appears together with its negative.
All inputs are finite; a program needn't handle non-finite values.
Results may differ from a plain program's by a relative error of at most 0.0047.
Values may be sent and summed in bfloat16 or wider, within the bound.
A program may use at most 128 MiB of HBM per device.

v0:
```python
import functools
import math

import jax
import jax.numpy as jnp
from jax import lax
from jax.experimental import pallas as pl
from jax.experimental.pallas import tpu as pltpu
from jax.sharding import PartitionSpec as P

BOX = 64
TILE = 256
SIN = (6.2831853, -41.3417004, 81.6051314, -76.7030154, 42.025927, -14.8998467, 3.23813751)
COS = (0.999999989, -19.7392045, 64.9391175, -85.4501395, 60.167631, -25.9675992, 6.52865816)


def horner(coeffs, u):
    total = coeffs[-1] * u + coeffs[-2]
    for c in coeffs[-3::-1]:
        total = total * u + c
    return total


def over(a, b, dims):
    return lax.dot_general(a, b, (dims, ((), ())), preferred_element_type=jnp.float32)


def kernel(
    n, parts, total_atoms,
    pos_ref, feat_ref, cot_ref, filt_ref, wcol_ref, wrow_ref,
    gfeat_ref, gpos_ref, gfilt_ref,
    cos_s, sin_s, src, recv, staged, full, grad_t, grad, grad_in, gp, gp_out, gp_in,
    rs_send, rs_recv, ag_send, ag_recv, w_send, w_recv,
):
    stages = n.bit_length() - 1
    waves = filt_ref.shape[0]
    atoms = feat_ref.shape[0]
    rows = waves // parts
    half = atoms // 2
    me = lax.axis_index("atom")
    core = lax.axis_index("wave")
    bits = [lax.rem(me // (1 << b), 2) for b in range(stages)]
    partners = [me + (1 - 2 * bits[b]) * (1 << b) for b in range(stages)]

    barrier = pltpu.get_barrier_semaphore()
    for partner in partners:
        pl.semaphore_signal(
            barrier, inc=1, device_id={"atom": partner}, device_id_type=pl.DeviceIdType.MESH
        )
    pl.semaphore_signal(
        barrier, inc=1, device_id={"wave": 1 - core}, device_id_type=pl.DeviceIdType.MESH
    )

    def order(p):
        return list(range(stages)) if p % 2 == 0 else list(range(1, stages)) + [0]

    def region(p, s):
        return p * rows + rows - (rows >> s)

    def remote(src_ref, dst_ref, send, recv_sem, axis, target):
        return pltpu.make_async_remote_copy(
            src_ref=src_ref, dst_ref=dst_ref, send_sem=send, recv_sem=recv_sem,
            device_id={axis: target}, device_id_type=pl.DeviceIdType.MESH,
        )

    def scatter_copy(p, s):
        where = pl.ds(region(p, s), rows >> (s + 1))
        return remote(
            staged.at[where], recv.at[where],
            rs_send.at[p * stages + s], rs_recv.at[p * stages + s], "atom",
            partners[order(p)[s]],
        )

    def stage(p, s):
        size = rows >> (s + 1)
        base = p * rows if s == 0 else offset(p, s - 1)
        start = base + (1 - bits[order(p)[s]]) * size
        step = min(size, 32)

        def narrow(i, _):
            a = src[pl.ds(pl.multiple_of(start + i * step, 16), step), :]
            to = pl.ds(pl.multiple_of(region(p, s) + i * step, 16), step)
            staged[to, :] = a.astype(jnp.bfloat16)
            return 0

        lax.fori_loop(0, size // step, narrow, 0)

    def offset(p, s):
        off = p * rows
        for j in range(s + 1):
            off = off + bits[order(p)[j]] * (rows >> (j + 1))
        return pl.multiple_of(off, 16)

    def gather_copy(p, s):
        size = rows >> (s + 1)
        where = pl.ds(offset(p, s), size)
        return remote(
            full.at[where], full.at[where],
            ag_send.at[p * stages + s], ag_recv.at[p * stages + s], "atom",
            partners[order(p)[s]],
        )

    p0 = pos_ref[0:1, :]
    p1 = pos_ref[1:2, :]
    p2 = pos_ref[2:3, :]

    def phase(i, _):
        at = pl.ds(pl.multiple_of(i * 16, 16), 16)
        w = wcol_ref[at, :]
        turns = w[:, 0:1] * p0 + w[:, 1:2] * p1 + w[:, 2:3] * p2
        frac = turns - jnp.round(turns)
        u = frac * frac
        sin_s[at, :] = horner(SIN, u) * frac
        cos_s[at, :] = horner(COS, u)
        return 0

    def forward(j, _):
        lax.fori_loop(j * (TILE // 16), (j + 1) * (TILE // 16), phase, 0)
        at = pl.ds(pl.multiple_of(j * TILE, TILE), TILE)
        channels = feat_ref.shape[1]
        c = cos_s[at, :].astype(jnp.bfloat16)
        s = sin_s[at, :].astype(jnp.bfloat16)
        nn = ((1,), (0,))
        for k, (wave, data) in enumerate(
            ((c, feat_ref), (s, feat_ref), (c, cot_ref), (s, cot_ref))
        ):
            src[at, k * channels:(k + 1) * channels] = over(wave, data[...], nn)
        return 0

    def backward(j, _):
        at = pl.ds(pl.multiple_of(j * TILE, TILE), TILE)
        channels = feat_ref.shape[1]
        s_cos, s_sin, a_cos, a_sin = [
            full[at, k * channels:(k + 1) * channels].astype(jnp.float32) for k in range(4)
        ]
        gfilt_ref[at, :] = (s_cos * a_cos + s_sin * a_sin) * (1.0 / total_atoms)
        filt = filt_ref[at, :] * (1.0 / total_atoms)
        f_sc = (filt * s_cos).astype(jnp.bfloat16)
        f_ss = (filt * s_sin).astype(jnp.bfloat16)
        f_ac = (filt * a_cos).astype(jnp.bfloat16)
        f_as = (filt * a_sin).astype(jnp.bfloat16)
        c = cos_s[at, :].astype(jnp.bfloat16)
        s = sin_s[at, :].astype(jnp.bfloat16)
        nt = ((1,), (1,))
        tn = ((0,), (0,))
        grad_t[...] += over(f_ac, c, tn) + over(f_as, s, tn)
        for h in range(2):
            cut = slice(h * half, (h + 1) * half)
            cot = cot_ref[cut, :]
            feat = feat_ref[cut, :]
            pcoef = over(f_sc, cot, nt) + over(f_ac, feat, nt)
            qcoef = over(f_ss, cot, nt) + over(f_as, feat, nt)
            dtheta = (
                cos_s[at, cut] * qcoef
                - sin_s[at, cut] * pcoef
            ).astype(jnp.bfloat16)
            gp[h] += over(wrow_ref[j], dtheta, ((1,), (0,)))
        return 0

    tiles = rows // TILE
    copies = []
    for p in range(parts):
        lax.fori_loop(p * tiles, (p + 1) * tiles, forward, 0)
        if p == 0:
            pl.semaphore_wait(barrier, stages + 1)
        stage(p, 0)
        copy = scatter_copy(p, 0)
        copy.start()
        copies.append(copy)
    grad_t[...] = jnp.zeros_like(grad_t)
    gp[...] = jnp.zeros_like(gp)

    for s in range(stages):
        for p in range(parts):
            scatter_copy(p, s).wait_recv()
            size = rows >> (s + 1)
            last = s == stages - 1
            mine = offset(p, s)
            step = min(size, 32)

            def add(i, _, mine=mine, last=last, step=step, came=region(p, s)):
                at = pl.ds(pl.multiple_of(mine + i * step, 16), step)
                b = recv[pl.ds(pl.multiple_of(came + i * step, 16), step), :]
                total = src[at, :] + b.astype(jnp.float32)
                if last:
                    full[at, :] = total.astype(jnp.bfloat16)
                else:
                    src[at, :] = total
                return 0

            lax.fori_loop(0, size // step, add, 0)
            if not last:
                stage(p, s + 1)
            copy = gather_copy(p, s) if last else scatter_copy(p, s + 1)
            copy.start()
            copies.append(copy)

    for s in reversed(range(stages)):
        for p in range(parts):
            gather_copy(p, s).wait_recv()
            if s > 0:
                copy = gather_copy(p, s - 1)
                copy.start()
                copies.append(copy)
            else:
                lax.fori_loop(p * tiles, (p + 1) * tiles, backward, 0)

    grad[...] = grad_t[...].T
    factor = 2.0 * math.pi / BOX
    gp_out[...] = gp[...] * factor
    other = pl.multiple_of((1 - core) * half, half)
    own = pl.multiple_of(core * half, half)
    give = remote(
        grad.at[pl.ds(other, half)], grad_in, w_send.at[0], w_recv.at[0], "wave", 1 - core
    )
    give_pos = remote(
        gp_out.at[1 - core], gp_in, w_send.at[1], w_recv.at[1], "wave", 1 - core
    )
    give.start()
    give_pos.start()
    for copy in copies:
        copy.wait_send()
    give.wait_recv()
    give_pos.wait_recv()
    gfeat_ref[...] = grad[pl.ds(own, half), :] + grad_in[...]
    gpos_ref[...] = gp_out[core] + gp_in[...]
    give.wait_send()
    give_pos.wait_send()


def per_device(positions, features, cotangent, filters, wave_ints):
    n = lax.axis_size("atom")
    atoms, channels = features.shape
    waves = filters.shape[0]
    stages = n.bit_length() - 1
    parts = max(1, min(4, waves // (16 * n)))
    total_atoms = atoms * n
    half = atoms // 2
    scaled = positions * (1.0 / BOX)
    columns = wave_ints.astype(jnp.float32).T
    triples = jnp.pad(wave_ints.astype(jnp.bfloat16), ((0, 13), (0, 0)))
    triples = triples.reshape(16, waves // TILE, TILE).transpose(1, 0, 2)
    vmem = pl.BlockSpec(memory_space=pltpu.VMEM)
    bf16, f32 = jnp.bfloat16, jnp.float32
    count = parts * stages
    grad_features, grad_positions, grad_filter = pl.pallas_call(
        functools.partial(kernel, n, parts, total_atoms),
        out_shape=(
            jax.ShapeDtypeStruct((half, channels), f32),
            jax.ShapeDtypeStruct((16, half), f32),
            jax.ShapeDtypeStruct((waves, channels), f32),
        ),
        in_specs=[vmem] * 6,
        out_specs=(vmem, vmem, vmem),
        scratch_shapes=[
            pltpu.VMEM((waves, atoms), f32),
            pltpu.VMEM((waves, atoms), f32),
            pltpu.VMEM((waves, 4 * channels), f32),
            pltpu.VMEM((waves, 4 * channels), bf16),
            pltpu.VMEM((waves, 4 * channels), bf16),
            pltpu.VMEM((waves, 4 * channels), bf16),
            pltpu.VMEM((channels, atoms), f32),
            pltpu.VMEM((atoms, channels), f32),
            pltpu.VMEM((half, channels), f32),
            pltpu.VMEM((2, 16, half), f32),
            pltpu.VMEM((2, 16, half), f32),
            pltpu.VMEM((16, half), f32),
            pltpu.SemaphoreType.DMA((count,)),
            pltpu.SemaphoreType.DMA((count,)),
            pltpu.SemaphoreType.DMA((count,)),
            pltpu.SemaphoreType.DMA((count,)),
            pltpu.SemaphoreType.DMA((2,)),
            pltpu.SemaphoreType.DMA((2,)),
        ],
        compiler_params=pltpu.CompilerParams(
            collective_id=0, has_side_effects=True, vmem_limit_bytes=56 * 1024 * 1024
        ),
    )(scaled, features, cotangent, filters, columns, triples)
    return (grad_features, grad_positions[:3], grad_filter)


def solution(mesh):
    placed = (
        P(None, ("group", "atom")),
        P(("group", "atom"), None),
        P(("group", "atom"), None),
        P("wave", None),
        P(None, "wave"),
    )
    return jax.shard_map(
        per_device,
        mesh=mesh,
        in_specs=placed,
        out_specs=(
            P(("group", "atom", "wave"), None),
            P(None, ("group", "atom", "wave")),
            P(("group", "wave"), None),
        ),
        check_vma=False,
    )
```

profile of v0, /device:TPU:0, one launch (start us, length us, event | category | flops | bytes accessed | tf_op | source)
XLA Modules:
  0.0 146.0 jit_solution(3738897021026577838)
XLA Ops:
  0.6 1.3 broadcast_multiply_fusion.pos_ref
  2.0 0.8 fusion
  2.8 0.6 copy.13
  3.5 1.3 copy.9
  4.8 135.0 %shard_map.76 = (f32[512,256]{1,0:T(8,128)}, f32[16,512]{1,0:T(8,128)}, f32[2048,256]{1,0:T(8,128)}) custom-call(f32[3,1024]{1,0:T(4,128)} %broadcast_multiply_fusion.pos_ref, bf16[1024,256]{1,0:T(8,128)(2,1)} %feat_ref.1, bf16[1024,256]{1,0:T(8,128)(2,1)} %cot_ref.1, f32[2048,256]{1,0:T(8,128)} %filt_ref.1, f32[2048,3]{1,0:T(8,128)} %bitcast.8, ...), custom_call_target="tpu_custom_call" | custom-call | tf_op jit(solution)/shard_map/pallas_call | solution.py:246
  139.8 1.3 slice.3
  141.1 1.9 %copy.16 = f32[512,256]{1,0:T(8,128)} copy(f32[512,256]{1,0:T(8,128)} %get-tuple-element.14) | data formatting | bytes 1048576
  142.9 3.0 %copy.17 = f32[2048,256]{1,0:T(8,128)} copy(f32[2048,256]{1,0:T(8,128)} %get-tuple-element.16) | data formatting | bytes 4194304
  (1 shorter events, 0.0 us)
where the time goes:
time: 146 us
  Pallas kernels  135 us (92%)
  local copies, waits for them, and re-layouts  8.21 us (6%)
  other arithmetic  2.17 us (1%)
    pallas_call x1, Pallas kernels, per_device(): pl.pallas_call(functools.partial(kernel, n, parts, total_atoms), out_shap...  135 us
    unnamed x2, local copies, waits for them, and re-layouts  4.91 us

commit v1 on v0

--- a/solution.py
+++ b/solution.py
@@ -233,7 +233,7 @@
     atoms, channels = features.shape
     waves = filters.shape[0]
     stages = n.bit_length() - 1
-    parts = max(1, min(4, waves // (16 * n)))
+    parts = max(1, min(8, waves // (16 * n)))
     total_atoms = atoms * n
     half = atoms // 2
     scaled = positions * (1.0 / BOX)

time: 146 us -> 137 us (0.938)
  Pallas kernels: 135 us -> 126 us
    pallas_call x1, Pallas kernels: 135 us -> 126 us  [per_device(): pl.pallas_call(functools.partial(kernel, n, parts, total_atoms), out_shap...]
where the time goes in v1:
time: 137 us
  Pallas kernels  126 us (92%)
  local copies, waits for them, and re-layouts  8.21 us (6%)
  other arithmetic  2.17 us (2%)
    pallas_call x1, Pallas kernels, per_device(): pl.pallas_call(functools.partial(kernel, n, parts, total_atoms), out_shap...  126 us
    unnamed x2, local copies, waits for them, and re-layouts  4.91 us

profile of v1, /device:TPU:0, one launch (start us, length us, event | category | flops | bytes accessed | tf_op | source)
XLA Modules:
  0.0 136.5 jit_solution(4341485214594904992)
XLA Ops:
  0.6 1.3 broadcast_multiply_fusion.pos_ref
  2.0 0.8 fusion
  2.8 0.6 copy.13
  3.5 1.3 copy.9
  4.8 125.5 %shard_map.76 = (f32[512,256]{1,0:T(8,128)}, f32[16,512]{1,0:T(8,128)}, f32[2048,256]{1,0:T(8,128)}) custom-call(f32[3,1024]{1,0:T(4,128)} %broadcast_multiply_fusion.pos_ref, bf16[1024,256]{1,0:T(8,128)(2,1)} %feat_ref.1, bf16[1024,256]{1,0:T(8,128)(2,1)} %cot_ref.1, f32[2048,256]{1,0:T(8,128)} %filt_ref.1, f32[2048,3]{1,0:T(8,128)} %bitcast.8, ...), custom_call_target="tpu_custom_call" | custom-call | tf_op jit(solution)/shard_map/pallas_call | solution.py:246
  130.3 1.3 slice.3
  131.6 1.9 %copy.16 = f32[512,256]{1,0:T(8,128)} copy(f32[512,256]{1,0:T(8,128)} %get-tuple-element.14) | data formatting | bytes 1048576
  133.5 3.0 %copy.17 = f32[2048,256]{1,0:T(8,128)} copy(f32[2048,256]{1,0:T(8,128)} %get-tuple-element.16) | data formatting | bytes 4194304
  (1 shorter events, 0.0 us)
